TPU v7x, 32 devices: a whole 2x2x4 slice. The times are simulated.
32 devices in a mesh: gy: 8 (over y, x, core), gx: 4 (over z).
Axes of the slice: x: 2, y: 2, z: 4, core: 2. Of those that a mesh axis runs over, the one named last changes fastest.
Arguments:
- velocity: bfloat16 [3, 32, 1536, 1536], P(None, 'gy', 'gx'), may hold values from -40 to 40
- ref_planes: int32 [6], replicated, may hold values from 4 to 27, as said below
- partner_offsets: int32 [8], replicated, may hold values from -4 to 4, as said below
- band_owner: int32 [48], replicated, may hold values from 0 to 7, as said below
Outputs:
- correlations: float32 [96, 9, 384, 384], P('gy', None, 'gx')
Inputs may be any that keep to these rules, and one draw needn't show every extreme that they name: `ref_planes`: 6 distinct planes; 4 and 27 are among them. `partner_offsets`: 8 distinct offsets; -4 and 4 are among them. `band_owner`: the pairs owned by one index of gy are consecutive; no index owns more than 12 pairs and one owns exactly 12.
All inputs are finite; a program needn't handle non-finite values.
Results may differ from a plain program's by a relative error of at most 0.0035.
Values may be sent and summed in bfloat16 or wider, within the bound.
A program may use at most 256 MiB of HBM per device.

v0:
```python
import math

import jax
import jax.numpy as jnp
from jax import lax
from jax.sharding import PartitionSpec as P


def angle_table(count_rows, count_cols, length):
    rows = jnp.arange(count_rows, dtype=jnp.int32)
    cols = jnp.arange(count_cols, dtype=jnp.int32)
    phase = rows[:, None] * cols[None, :] % length
    return 2.0 * math.pi / length * phase.astype(jnp.float32)


def x_transform(received, cos_x, sin_x):
    width_x = received.shape[-1]
    flat_rows = received.reshape(-1, width_x)
    cosine_part = jnp.dot(flat_rows, cos_x, preferred_element_type=jnp.float32).reshape(
        received.shape
    )
    sine_part = jnp.dot(flat_rows, sin_x, preferred_element_type=jnp.float32).reshape(
        received.shape
    )
    real_part = cosine_part[:, :, 0] + sine_part[:, :, 1]
    imag_part = cosine_part[:, :, 1] - sine_part[:, :, 0]
    return (real_part, imag_part)


def spread_left(left):
    return left.transpose(1, 0, 2, 3, 4, 5)[:, None, :, None]


def spread_right(right):
    return right.transpose(1, 2, 0, 3, 4, 5, 6)[:, :, None]


def per_device(velocity, ref_planes, partner_offsets, band_owner):
    highest = lax.Precision.HIGHEST
    row_count = lax.axis_size("gy")
    col_count = lax.axis_size("gx")
    devices = row_count * col_count
    comp_count, planes_dev, x_dev, width_z = velocity.shape
    width_x = x_dev * col_count
    half = width_z // 2
    lag_z = width_z // 4
    lag_x = width_x // 4
    block_len = lag_z // devices
    lag_block = lag_x // col_count
    row_id = lax.axis_index("gy")
    col_id = lax.axis_index("gx")
    norm_scale = 1.0 / float(width_x * width_z) ** 2
    z_angle = angle_table(width_z, half, width_z)
    forward_z = jnp.concatenate([jnp.cos(z_angle), -jnp.sin(z_angle)], axis=1).astype(jnp.bfloat16)
    x_angle = angle_table(width_x, width_x, width_x)
    cos_x = jnp.cos(x_angle).astype(jnp.bfloat16)
    sin_x = jnp.sin(x_angle).astype(jnp.bfloat16)
    along_z = jnp.einsum("cpxz,zq->cpqx", velocity, forward_z, preferred_element_type=jnp.float32)
    along_z = along_z.astype(jnp.bfloat16).reshape(comp_count, planes_dev, 2, 2, lag_z, x_dev)
    parcels = along_z.reshape(comp_count, planes_dev, 2, 2, devices, block_len, x_dev)
    parcels = parcels.transpose(4, 0, 1, 2, 3, 5, 6)
    item_rows = lax.all_to_all(parcels, ("gy", "gx"), split_axis=0, concat_axis=0, tiled=True)
    item_count = item_rows.shape[1]
    grouped = item_rows.reshape(
        row_count, col_count, item_count, planes_dev, 2, 2, block_len, x_dev
    )
    grouped = grouped.transpose(2, 0, 3, 4, 5, 6, 1, 7)
    grouped = grouped.reshape(item_count, row_count * planes_dev, 2, 2, block_len, width_x)
    real_part, imag_part = x_transform(grouped, cos_x, sin_x)
    block_start = (row_id * col_count + col_id) * block_len
    mode_index = (
        jnp.arange(2, dtype=jnp.int32)[:, None] * lag_z
        + block_start
        + jnp.arange(block_len, dtype=jnp.int32)[None, :]
    )
    weight = jnp.where(mode_index == 0, 1.0, 2.0).astype(jnp.float32)[None, None, :, :, None]
    ref_count = ref_planes.shape[0]
    off_count = partner_offsets.shape[0]
    pair_count = ref_count * off_count
    partner_index = (ref_planes[:, None] + partner_offsets[None, :]).reshape(-1)
    ref_real = (jnp.take(real_part, ref_planes, axis=1) * weight).reshape(
        comp_count, ref_count, 2, block_len, 4, lag_x
    )
    ref_imag = (jnp.take(imag_part, ref_planes, axis=1) * weight).reshape(
        comp_count, ref_count, 2, block_len, 4, lag_x
    )
    part_real = jnp.take(real_part, partner_index, axis=1).reshape(
        comp_count, ref_count, off_count, 2, block_len, 4, lag_x
    )
    part_imag = jnp.take(imag_part, partner_index, axis=1).reshape(
        comp_count, ref_count, off_count, 2, block_len, 4, lag_x
    )
    left_real = spread_left(ref_real)
    left_imag = spread_left(ref_imag)
    right_real = spread_right(part_real)
    right_imag = spread_right(part_imag)
    fold_real = jnp.sum(left_real * right_real + left_imag * right_imag, axis=(4, 6))
    fold_imag = jnp.sum(left_real * right_imag - left_imag * right_real, axis=(4, 6))
    fold_real = fold_real.reshape(pair_count, 9, block_len, lag_x)
    fold_imag = fold_imag.reshape(pair_count, 9, block_len, lag_x)
    slot_count = (2 * pair_count + row_count - 1) // row_count
    pair_order = jnp.arange(pair_count, dtype=jnp.int32)
    same_owner = band_owner[:, None] == band_owner[None, :]
    earlier = pair_order[None, :] < pair_order[:, None]
    slot_of = jnp.sum((same_owner & earlier).astype(jnp.int32), axis=1)
    dest_row = band_owner * slot_count + slot_of
    dest_table = (
        dest_row[None, :] == jnp.arange(row_count * slot_count, dtype=jnp.int32)[:, None]
    ).astype(jnp.float32)
    span_angle = angle_table(lag_z, lag_z, lag_z)
    cos_span = jnp.cos(span_angle).reshape(devices, block_len, lag_z)
    sin_span = jnp.sin(span_angle).reshape(devices, block_len, lag_z)
    lag_angle = angle_table(lag_x, lag_x, lag_x)
    cos_lag = jnp.cos(lag_angle)
    sin_lag = jnp.sin(lag_angle)
    lag_real = jnp.einsum("pqkx,xa->pqka", fold_real, cos_lag, precision=highest) - jnp.einsum(
        "pqkx,xa->pqka", fold_imag, sin_lag, precision=highest
    )
    lag_imag = jnp.einsum("pqkx,xa->pqka", fold_real, sin_lag, precision=highest) + jnp.einsum(
        "pqkx,xa->pqka", fold_imag, cos_lag, precision=highest
    )
    placed = jnp.dot(
        dest_table,
        jnp.stack([lag_real, lag_imag], axis=2).reshape(pair_count, -1),
        precision=highest,
    )
    placed = placed.reshape(row_count, slot_count, 9, 2, block_len, col_count, lag_block)
    placed = placed.transpose(0, 5, 1, 2, 3, 4, 6)
    buffer = placed.reshape(devices, slot_count, 9, 2, block_len * lag_block)
    arrived = lax.all_to_all(buffer, ("gy", "gx"), split_axis=0, concat_axis=0, tiled=True)
    arrived = arrived.reshape(devices, arrived.shape[1], 9, 2, block_len, lag_block)
    lagged = jnp.einsum("dsqkl,dkz->sqlz", arrived[:, :, :, 0], cos_span, precision=highest)
    lagged = lagged - jnp.einsum(
        "dsqkl,dkz->sqlz", arrived[:, :, :, 1], sin_span, precision=highest
    )
    return lagged * norm_scale


def solution(mesh):
    placed = (P(None, "gy", "gx", None), P(), P(), P())
    return jax.shard_map(
        per_device, mesh=mesh, in_specs=placed, out_specs=P("gy", None, "gx", None), check_vma=False
    )
```

profile of v0, /device:TPU:17, one launch (start us, length us, event | category | flops | bytes accessed | tf_op | source)
XLA Modules:
  0.0 2033.6 jit_solution(2285723793080775002)
XLA Ops:
  19.6 26.5 %convert_bitcast_fusion = bf16[3,4,1536,384]{3,2,1,0:T(8,128)(2,1)} fusion(bf16[3,4,384,1536]{3,2,1,0:T(8,128)(2,1)} %param.8, bf16[1536,768]{0,1:T(8,128)(2,1)S(1)} %get-tuple-element.17, bf16[1536,768]{0,1:T(8,128)(2,1)S(1)} %get-tuple-element.18), kind=kOutput, calls=%fused_computation.23 | convolution fusion | flops 21759787008 | bytes 33030144 | tf_op jit(solution)/shard_map/cpxz,zq->cpqx/dot_general | solution.py:58
  46.1 25.6 %copy.67 = bf16[3,4,1536,384]{3,1,2,0:T(4,128)(2,1)S(1)} copy(bf16[3,4,1536,384]{3,2,1,0:T(8,128)(2,1)} %convert_bitcast_fusion) | data formatting | bytes 28311552 | tf_op jit(solution)/shard_map/convert_element_type | solution.py:59
  89.0 36.7 %fusion.128 = bf16[1536,1536,1,1,1,1]{1,0,5,4,3,2:T(8,128)(2,1)} fusion(), kind=kLoop, calls=%fused_computation.38.clone.clone.1 | loop fusion | flops 23592960 | bytes 4718592 | tf_op jit(solution)/shard_map/dot_general | solution.py:19
  125.6 37.0 %fusion.130 = bf16[1536,1536,1,1,1,1]{1,0,5,4,3,2:T(8,128)(2,1)} fusion(), kind=kLoop, calls=%fused_computation.40.clone.clone.1 | loop fusion | flops 23592960 | bytes 4718592 | tf_op jit(solution)/shard_map/dot_general | solution.py:22
  162.6 235.2 %all-to-all-done = bf16[32,3,4,2,2,12,384]{6,2,5,4,3,1,0:T(4,128)(2,1)} async-done(((bf16[32,3,4,2,2,12,384]{6,2,5,4,3,1,0:T(4,128)(2,1)}), bf16[32,3,4,2,2,12,384]{6,2,5,4,3,1,0:T(4,128)(2,1)}, u32[]{:S(2)}, u32[]{:S(2)}) %all-to-all-start) | async-done | bytes 14155808 | tf_op jit(solution)/shard_map/all_to_all | solution.py:62
  410.7 23.5 %dot_general.37 = bf16[3,32,2,2,12,1536]{5,1,4,3,2,0:T(8,128)(2,1)} reshape(bf16[3,8,4,2,2,12,4,384]{7,6,2,1,5,4,3,0:T(4,128)(2,1)} %bitcast.146) | data formatting | bytes 28311552 | tf_op jit(solution)/shard_map/dot_general | solution.py:19
  434.2 29.3 %fusion.15 = f32[3,32,2,2,12,1536]{5,1,4,3,2,0:T(8,128)} fusion(bf16[3,32,2,2,12,1536]{5,1,4,3,2,0:T(8,128)(2,1)} %dot_general.37, bf16[1536,1536,1,1,1,1]{1,0,5,4,3,2:T(8,128)(2,1)} %fusion.128), kind=kOutput, calls=%fused_computation.39 | convolution fusion | flops 21743271936 | bytes 47185920 | tf_op jit(solution)/shard_map/dot_general | solution.py:19
  463.4 25.8 %fusion.18 = f32[3,32,2,2,12,1536]{5,1,4,3,2,0:T(8,128)} fusion(bf16[3,32,2,2,12,1536]{5,1,4,3,2,0:T(8,128)(2,1)S(1)} %copy-done.3, bf16[1536,1536,1,1,1,1]{1,0,5,4,3,2:T(8,128)(2,1)S(1)} %bitcast.148), kind=kOutput, calls=%fused_computation.41 | convolution fusion | flops 21743271936 | bytes 47185920 | tf_op jit(solution)/shard_map/dot_general | solution.py:22
  489.2 25.4 %fusion.6 = (f32[3,32,2,12,1536]{4,1,3,2,0:T(8,128)}, f32[3,32,2,12,1536]{4,1,3,2,0:T(8,128)S(1)}) fusion(f32[3,32,2,2,12,1536]{5,1,4,3,2,0:T(8,128)} %fusion.18, f32[3,32,2,2,12,1536]{5,1,4,3,2,0:T(8,128)} %fusion.15), kind=kLoop, calls=%fused_computation.21 | loop fusion | flops 7077888 | bytes 84934656 | tf_op jit(solution)/shard_map/add | solution.py:25
  514.6 24.4 %copy.70 = f32[3,32,2,12,1536]{4,2,3,1,0:T(2,128)} copy(f32[3,32,2,12,1536]{4,1,3,2,0:T(8,128)} %get-tuple-element.11) | data formatting | bytes 28311552 | tf_op jit(solution)/shard_map/add | solution.py:25
  553.5 38.1 %gather_fusion.1 = f32[48,3,2,12,1536]{4,2,3,1,0:T(2,128)} fusion(f32[3,32,2,12,1536]{4,2,3,1,0:T(2,128)} %copy.70, s32[1024]{0:T(1024)} %pad_clamp_fusion), kind=kCustom, calls=%fused_computation.1.clone | custom fusion | bytes 42467520 | tf_op jit(solution)/shard_map/jit(_take)/gather | solution.py:87
  591.7 38.4 %gather_fusion.3 = f32[48,3,2,12,1536]{4,2,3,1,0:T(2,128)} fusion(f32[3,32,2,12,1536]{4,2,3,1,0:T(2,128)} %copy.75, s32[1024]{0:T(1024)} %pad_clamp_fusion), kind=kCustom, calls=%fused_computation.3.clone | custom fusion | bytes 42467520 | tf_op jit(solution)/shard_map/jit(_take)/gather | solution.py:90
  648.8 28.8 %select_bitcast_fusion.1 = (f32[3,48,2,12,1536]{4,2,3,0,1:T(2,128)}, f32[3,48,2,12,1536]{4,2,3,0,1:T(2,128)}) fusion(f32[48,3,2,12,1536]{4,2,3,1,0:T(2,128)} %gather_fusion.1, pred[48]{0:T(512)(128)(4,1)S(1)} %copy-done.7, f32[48,3,2,12,1536]{4,2,3,1,0:T(2,128)} %gather_fusion.3), kind=kLoop, calls=%fused_computation.14 | loop fusion | flops 10616832 | bytes 84934704 | tf_op jit(solution)/shard_map/jit(_take)/select_n | solution.py:87
  677.6 29.1 %reshape.186 = f32[3,6,8,2,12,4,384]{6,5,3,4,0,2,1:T(4,128)} reshape(f32[3,48,2,12,1536]{4,2,3,0,1:T(2,128)} %get-tuple-element.15) | data formatting | bytes 42467328 | tf_op jit(solution)/shard_map/reshape | solution.py:87
  728.2 28.9 %reshape.188 = f32[3,6,8,2,12,4,384]{6,5,3,4,0,2,1:T(4,128)} reshape(f32[3,48,2,12,1536]{4,2,3,0,1:T(2,128)} %get-tuple-element.16) | data formatting | bytes 42467328 | tf_op jit(solution)/shard_map/reshape | solution.py:90
  793.9 43.1 %subtract_reduce_fusion = (f32[6,8,3,3,12,384]{5,1,4,3,2,0:T(8,128)}, f32[6,8,3,3,12,384]{5,1,4,3,2,0:T(8,128)S(1)}) fusion(f32[6,8,3,2,12,4,384]{6,1,5,4,3,2,0:T(8,128)} %copy.79, f32[6,8,3,2,12,4,384]{6,1,5,4,3,2,0:T(8,128)} %copy.74, f32[3,6,2,12,4,384]{5,4,2,3,0,1:T(4,128)S(1)} %reshape.249, f32[3,6,2,12,4,384]{5,4,2,3,0,1:T(4,128)} %reshape.250), kind=kLoop, calls=%fused_computation.4 | loop fusion | flops 123420672 | bytes 63700992 | tf_op jit(solution)/shard_map/reduce_sum | solution.py:98
  981.1 33.2 %convolution_bitcast_fusion = f32[8,4,12,9,2,12,96]{6,2,1,5,4,3,0:T(8,128)} fusion(f32[9,2,12,4,96,48]{4,3,2,1,0,5:T(4,128)} %dot_general.45, s32[8,12]{1,0:T(8,128)S(1)} %copy-done.4, s32[48]{0:T(128)S(1)} %copy-done.5), kind=kOutput, calls=%fused_computation.6 | convolution fusion | flops 4586476032 | bytes 47776320 | tf_op jit(solution)/shard_map/dot_general | solution.py:122
  1014.3 41.0 %copy.103 = f32[8,4,12,9,2,12,96]{6,5,4,3,2,1,0:T(8,128)} copy(f32[8,4,12,9,2,12,96]{6,2,1,5,4,3,0:T(8,128)} %convolution_bitcast_fusion) | data formatting | bytes 63700992 | tf_op jit(solution)/shard_map/reshape | solution.py:129
  1055.3 57.4 %reshape.251 = f32[32,12,9,2,1152]{4,3,2,1,0:T(2,128)} reshape(f32[8,4,12,9,2,12,96]{6,5,4,3,2,1,0:T(8,128)} %copy.103) | data formatting | bytes 63700992 | tf_op jit(solution)/shard_map/reshape | solution.py:129
  1116.7 706.6 %all-to-all-done.1 = f32[32,12,9,2,1152]{4,3,2,1,0:T(2,128)} async-done(((f32[32,12,9,2,1152]{4,3,2,1,0:T(2,128)}), f32[32,12,9,2,1152]{4,3,2,1,0:T(2,128)}, u32[]{:S(2)}, u32[]{:S(2)}) %all-to-all-start.1) | async-done | bytes 31850528 | tf_op jit(solution)/shard_map/all_to_all | solution.py:130
  1823.3 59.4 %reshape.252 = f32[32,12,9,2,12,96]{5,4,3,2,1,0:T(8,128)} reshape(f32[32,12,9,2,1152]{4,3,2,1,0:T(2,128)} %all-to-all-done.1) | data formatting | bytes 63700992 | tf_op jit(solution)/shard_map/reshape | solution.py:131
  1882.7 37.5 %fusion.110 = (f32[32,12,9,1,12,96]{5,4,3,2,1,0:T(8,128)}, f32[32,12,9,1,12,96]{5,4,3,2,1,0:T(8,128)}) fusion(f32[32,12,9,2,12,96]{5,4,3,2,1,0:T(8,128)} %reshape.252), kind=kLoop, calls=%fused_computation.142 | loop fusion | bytes 63700992 | tf_op jit(solution)/shard_map/slice | solution.py:132
  1920.1 55.9 %fusion = f32[12,9,96,384,1]{3,2,4,1,0:T(8,128)} fusion(f32[32,12,9,1,12,96]{5,4,3,2,1,0:T(8,128)} %get-tuple-element.10, s32[32,12]{0,1:T(8,128)S(1)} %multiply_add_fusion), kind=kOutput, calls=%fused_computation.8 | convolution fusion | flops 18347212800 | bytes 31852032 | tf_op jit(solution)/shard_map/dsqkl,dkz->sqlz/dot_general | solution.py:133
  1976.0 57.2 %fusion.4 = f32[12,9,96,384]{3,2,1,0:T(8,128)} fusion(f32[12,9,96,384,1]{3,2,4,1,0:T(8,128)} %fusion, f32[32,12,9,1,12,96]{5,4,3,2,1,0:T(8,128)S(1)} %copy-done, s32[32,12]{0,1:T(8,128)S(1)} %multiply_add_fusion), kind=kOutput, calls=%fused_computation.17 | convolution fusion | flops 18355175424 | bytes 47777280 | tf_op jit(solution)/shard_map/dsqkl,dkz->sqlz/dot_general | solution.py:132
  (66 shorter events, 289.1 us)
Async XLA Ops:
  77.9 6.7 copy-start.9
  77.9 6.7 copy-start.10
  77.9 8.7 copy-start.11
  77.9 319.9 %all-to-all-start = ((bf16[32,3,4,2,2,12,384]{6,2,5,4,3,1,0:T(4,128)(2,1)}), bf16[32,3,4,2,2,12,384]{6,2,5,4,3,1,0:T(4,128)(2,1)}, u32[]{:S(2)}, u32[]{:S(2)}) async-start(bf16[32,3,4,2,2,12,384]{6,2,5,4,3,1,0:T(4,128)(2,1)} %copy.68), calls=%async_computation | async-start | bytes 28311552 | tf_op jit(solution)/shard_map/all_to_all | solution.py:62
  410.7 52.7 %slice-start = ((s8[4718592]{0:T(1024)(128)(4,1)}), s8[524288]{0:T(1024)(128)(4,1)S(1)}, s32[]{:S(2)}) async-start(s8[4718592]{0:T(1024)(128)(4,1)} %bitcast.147), calls=%async_computation.2 | async-start | bytes 1048576
  434.2 29.3 %copy-start.3 = (bf16[3,32,2,2,12,1536]{5,1,4,3,2,0:T(8,128)(2,1)S(1)}, bf16[3,32,2,2,12,1536]{5,1,4,3,2,0:T(8,128)(2,1)}, u32[]{:S(2)}) copy-start(bf16[3,32,2,2,12,1536]{5,1,4,3,2,0:T(8,128)(2,1)} %dot_general.37) | copy-start | bytes 42467332
  434.2 29.3 %slice-start.1 = ((s8[4718592]{0:T(1024)(128)(4,1)}), s8[4194304]{0:T(1024)(128)(4,1)S(1)}, s32[]{:S(2)}) async-start(s8[4718592]{0:T(1024)(128)(4,1)} %bitcast.147), calls=%async_computation.3 | async-start | bytes 8388608
  630.1 18.7 copy-start.7
  757.1 21.7 %copy-start.2 = (f32[6,3,2,12,1536]{4,2,3,1,0:T(2,128)S(1)}, f32[6,3,2,12,1536]{4,2,3,1,0:T(2,128)}, u32[]{:S(2)}) copy-start(f32[6,3,2,12,1536]{4,2,3,1,0:T(2,128)} %gather_fusion.2) | copy-start | bytes 7962628
  757.1 21.7 %copy-start.6 = (f32[2,12]{0,1:T(8,128)S(1)}, f32[2,12]{0,1:T(8,128)}, u32[]{:S(2)}) copy-start(f32[2,12]{0,1:T(8,128)} %fusion.84) | copy-start | bytes 292
  757.1 21.7 %copy-start.8 = (pred[6]{0:T(512)(128)(4,1)S(1)}, pred[6]{0:T(512)(128)(4,1)}, u32[]{:S(2)}) copy-start(pred[6]{0:T(512)(128)(4,1)} %compare_and_fusion.1) | copy-start | bytes 22
  907.0 21.6 %copy-start.1 = (f32[48,9,1,12,384]{4,0,3,1,2:T(8,128)S(1)}, f32[48,9,1,12,384]{4,0,3,1,2:T(8,128)}, u32[]{:S(2)}) copy-start(f32[48,9,1,12,384]{4,0,3,1,2:T(8,128)} %subtract_bitcast_fusion) | copy-start | bytes 23887876
  961.0 20.1 copy-start.4
  961.0 20.1 copy-start.5
  1112.7 710.6 %all-to-all-start.1 = ((f32[32,12,9,2,1152]{4,3,2,1,0:T(2,128)}), f32[32,12,9,2,1152]{4,3,2,1,0:T(2,128)}, u32[]{:S(2)}, u32[]{:S(2)}) async-start(f32[32,12,9,2,1152]{4,3,2,1,0:T(2,128)} %reshape.251), calls=%async_computation.1 | async-start | bytes 63700992 | tf_op jit(solution)/shard_map/all_to_all | solution.py:130
  1920.1 55.9 %copy-start = (f32[32,12,9,1,12,96]{5,4,3,2,1,0:T(8,128)S(1)}, f32[32,12,9,1,12,96]{5,4,3,2,1,0:T(8,128)}, u32[]{:S(2)}) copy-start(f32[32,12,9,1,12,96]{5,4,3,2,1,0:T(8,128)} %get-tuple-element.9) | copy-start | bytes 47775748
where the time goes:
time: 2050 us; the launch traced here: 2030 us
  waiting for transfers between devices  942 us (46%)
  local copies, waits for them, and re-layouts  560 us (27%)
  matrix products  315 us (15%)
  other arithmetic  205 us (10%)
    all_to_all x1, waiting for transfers between devices, per_device(): lax.all_to_all(buffer, ('gy', 'gx'), split_axis=0, concat_axis=0, tiled=T...  707 us
    all_to_all x1, waiting for transfers between devices, per_device(): lax.all_to_all(parcels, ('gy', 'gx'), split_axis=0, concat_axis=0, tiled=...  235 us
    reshape x2, local copies, waits for them, and re-layouts, per_device(): buffer = placed.reshape(devices, slot_count, 9, 2, block_len * lag_block)  98.4 us
    reshape x1, local copies, waits for them, and re-layouts, per_device(): arrived.reshape(devices, arrived.shape[1], 9, 2, block_len, lag_block)  59.4 us
    dot_general x1, matrix products, per_device(): jnp.einsum('dsqkl,dkz->sqlz', arrived[:, :, :, 0], cos_span, precision=hi...  57.2 us
    dot_general x1, matrix products, per_device(): jnp.einsum('dsqkl,dkz->sqlz', arrived[:, :, :, 1], sin_span, precision=hi...  55.9 us
    transpose x2, local copies, waits for them, and re-layouts, spread_right(): return right.transpose(1, 2, 0, 3, 4, 5, 6)[:, :, None]  43.2 us
    reduce_sum x1, other arithmetic, per_device(): jnp.sum(left_real * right_imag - left_imag * right_real, axis=(4, 6))  43.1 us
  transfers between devices with their start and end apart: 2, of which 2 were waited for; matrix products, arithmetic and copies ran while one was open for 4% of the time, Pallas kernels for 0%

commit v1 on v0

v1 whole, which is shorter than its diff:
```python
import functools
import math

import jax
import jax.numpy as jnp
import numpy as np
from jax import lax
from jax.experimental import pallas as pl
from jax.experimental.pallas import tpu as pltpu
from jax.sharding import PartitionSpec as P

LANES = 128
ROWS = 8


def circle(rows, cols, length):
    phase = np.asarray(rows, np.int64)[:, None] * np.asarray(cols, np.int64)[None, :] % length
    return 2.0 * np.pi / length * phase


def mode_members(lag_z, slots):
    half = lag_z // 2
    k = np.arange(slots)
    mirror = np.where(k == 0, half, lag_z - k)
    members = np.stack([k, k + lag_z, mirror, mirror + lag_z])
    return members, k < half


def forward_z_table(width_z, lag_z, devices, block_len):
    members, used = mode_members(lag_z, devices * block_len)
    angle = circle(members.reshape(-1), np.arange(width_z), width_z)
    sign = np.repeat(np.array([-1.0, -1.0, 1.0, 1.0]), devices * block_len)[:, None]
    table = np.stack([np.cos(angle), sign * np.sin(angle)])
    table = table.reshape(2, 4, devices * block_len, width_z) * used[None, None, :, None]
    table = table.reshape(2, 4, devices, block_len, width_z).transpose(2, 0, 1, 3, 4)
    return table.reshape(-1, width_z).astype(np.float32).astype(jnp.bfloat16)


def span_table(lag_z, devices, block_len):
    slots = devices * block_len
    k = np.arange(slots)
    t = np.arange(lag_z)
    angle = circle(k, t, lag_z)
    real = np.cos(angle)
    imag = -np.sin(angle)
    imag[0] = np.cos(np.pi * t)
    table = np.stack([real, imag]) * (k < lag_z // 2)[None, :, None]
    table = table.reshape(2, devices, block_len, lag_z).transpose(2, 0, 1, 3)
    return table.reshape(-1, lag_z).astype(np.float32).astype(jnp.bfloat16)


def fold_kernel(
    comps, planes_dev, block_len, row_count, col_count, off_count,
    refs, offs, got, cos_ref, sin_ref, weight_ref, out, spec, lhs,
):
    part_rows = 4 * block_len
    group = 2 * part_rows
    x_dev = got.shape[2] // (comps * planes_dev)
    pairs = out.shape[1]
    spec[...] = jnp.zeros_like(spec)

    def transform(g, carry):
        for n in range(comps * planes_dev):
            for col in range(col_count):
                lhs[n * group : (n + 1) * group, col * x_dev : (col + 1) * x_dev] = got[
                    g * col_count + col, :, n * x_dev : (n + 1) * x_dev
                ]
        cosine = jnp.dot(lhs[...], cos_ref[...], preferred_element_type=jnp.float32)
        sine = jnp.dot(lhs[...], sin_ref[...], preferred_element_type=jnp.float32)
        for n in range(comps * planes_dev):
            comp, plane = n // planes_dev, n % planes_dev
            y = g * planes_dev + plane
            a = n * group
            b = a + part_rows
            parts = (
                cosine[a:b] + sine[b : b + part_rows],
                cosine[b : b + part_rows] - sine[a:b],
            )
            for ri in range(2):
                weighted = parts[ri] * weight_ref[...]
                for mem in range(4):
                    lo = mem * block_len
                    spec[ri, mem, y, comp, 0:block_len, :] = weighted[lo : lo + block_len]
                for mem in range(2):
                    lo = (mem + 2) * block_len
                    spec[ri, mem, y, comp, block_len : block_len + 1, :] = parts[ri][lo : lo + 1]
        return carry

    lax.fori_loop(0, row_count, transform, 0)

    def fold(pair, carry):
        left = refs[pair // off_count]
        right = left + offs[pair % off_count]
        real = [None] * (comps * comps)
        imag = [None] * (comps * comps)
        for mem in range(4):
            for m in range(4):
                lanes = slice(m * LANES, (m + 1) * LANES)
                lr = [spec[0, mem, left, c, :, lanes] for c in range(comps)]
                li = [spec[1, mem, left, c, :, lanes] for c in range(comps)]
                rr = [spec[0, mem, right, c, :, lanes] for c in range(comps)]
                rim = [spec[1, mem, right, c, :, lanes] for c in range(comps)]
                for i in range(comps):
                    for j in range(comps):
                        n = i * comps + j
                        re = lr[i] * rr[j] + li[i] * rim[j]
                        im = lr[i] * rim[j] - li[i] * rr[j]
                        real[n] = re if real[n] is None else real[n] + re
                        imag[n] = im if imag[n] is None else imag[n] + im
        for n in range(comps * comps):
            out[0, pair, n] = real[n]
            out[1, pair, n] = imag[n]
        return carry

    lax.fori_loop(0, pairs, fold, 0)


def spread_kernel(block_count, scale, count, got, table, out):
    width = got.shape[2] // block_count
    live = pl.program_id(0) < count[0]
    for n in range(got.shape[0]):
        block = got[n]
        stacked = jnp.concatenate(
            [block[:, i * width : (i + 1) * width] for i in range(block_count)], axis=0
        )
        lagged = lax.dot_general(
            stacked, table[...], (((0,), (0,)), ((), ())), preferred_element_type=jnp.float32
        )
        out[0, n] = jnp.where(live, lagged * scale, 0.0)


def per_device(velocity, ref_planes, partner_offsets, band_owner):
    row_count = lax.axis_size("gy")
    col_count = lax.axis_size("gx")
    devices = row_count * col_count
    comps, planes_dev, x_dev, width_z = velocity.shape
    width_x = x_dev * col_count
    lag_z = width_z // 4
    lag_x = width_x // 4
    lag_block = lag_x // col_count
    block_len = (lag_z // 2 + devices - 1) // devices
    row_id = lax.axis_index("gy")
    device_id = row_id * col_count + lax.axis_index("gx")
    first = device_id == 0
    norm_scale = 2.0 / float(width_x * width_z) ** 2
    refs = ref_planes.shape[0]
    offs = partner_offsets.shape[0]
    pairs = refs * offs
    squares = comps * comps
    planes = planes_dev * row_count

    table_z = jnp.asarray(forward_z_table(width_z, lag_z, devices, block_len))
    along_z = lax.dot_general(
        table_z,
        velocity.reshape(comps * planes_dev * x_dev, width_z),
        (((1,), (1,)), ((), ())),
        preferred_element_type=jnp.float32,
    ).astype(jnp.bfloat16)
    parcels = along_z.reshape(devices, 8 * block_len, comps * planes_dev * x_dev)
    got = lax.all_to_all(parcels, ("gy", "gx"), split_axis=0, concat_axis=0, tiled=True)

    tiles = lag_x // LANES
    angle_x = circle(np.arange(width_x), np.arange(width_x), width_x)
    angle_x = angle_x.reshape(width_x, 4, tiles, LANES).transpose(0, 2, 1, 3)
    angle_x = angle_x.reshape(width_x, width_x)
    cos_x = jnp.asarray(np.cos(angle_x).astype(np.float32).astype(jnp.bfloat16))
    sin_x = jnp.asarray(np.sin(angle_x).astype(np.float32).astype(jnp.bfloat16))

    plain = np.ones((4, block_len), np.float32)
    zero_mode = plain.copy()
    zero_mode[0, 0] = math.sqrt(0.5)
    zero_mode[2:, 0] = 0.0
    weight = jnp.where(first, zero_mode.reshape(-1), plain.reshape(-1))
    weight = jnp.broadcast_to(weight[:, None], (4 * block_len, 4 * LANES))

    lines = comps * planes_dev * 8 * block_len
    folded = pl.pallas_call(
        functools.partial(
            fold_kernel, comps, planes_dev, block_len, row_count, col_count, offs
        ),
        grid_spec=pltpu.PrefetchScalarGridSpec(
            num_scalar_prefetch=2,
            grid=(tiles,),
            in_specs=[
                pl.BlockSpec(got.shape, lambda t, *_: (0, 0, 0), pipeline_mode=pl.Buffered(1)),
                pl.BlockSpec((width_x, 4 * LANES), lambda t, *_: (0, t)),
                pl.BlockSpec((width_x, 4 * LANES), lambda t, *_: (0, t)),
                pl.BlockSpec((4 * block_len, 4 * LANES), lambda t, *_: (0, 0)),
            ],
            out_specs=pl.BlockSpec(
                (2, pairs, squares, ROWS, LANES), lambda t, *_: (0, 0, 0, 0, t)
            ),
            scratch_shapes=[
                pltpu.VMEM((2, 4, planes, comps, ROWS, 4 * LANES), jnp.float32),
                pltpu.VMEM((lines, width_x), jnp.bfloat16),
            ],
        ),
        out_shape=jax.ShapeDtypeStruct((2, pairs, squares, ROWS, lag_x), jnp.float32),
        compiler_params=pltpu.CompilerParams(vmem_limit_bytes=58 * 2**20),
        name="transform_and_fold",
    )(ref_planes, partner_offsets, got, cos_x, sin_x, weight)

    angle_lag = circle(np.arange(lag_x), np.arange(lag_x), lag_x).reshape(
        lag_x, col_count, 1, lag_block
    )
    from_real = np.concatenate([np.cos(angle_lag), np.sin(angle_lag)], axis=2)
    from_imag = np.concatenate([-np.sin(angle_lag), np.cos(angle_lag)], axis=2)
    from_real = from_real.reshape(lag_x, 2 * lag_x).astype(np.float32)
    from_imag = from_imag.reshape(lag_x, 2 * lag_x).astype(np.float32)
    flat = folded.reshape(2, pairs * squares * ROWS, lag_x)
    lags = jnp.dot(flat[0], from_real, precision=lax.Precision.HIGH) + jnp.dot(
        flat[1], from_imag, precision=lax.Precision.HIGH
    )
    lags = lags.astype(jnp.bfloat16).reshape(pairs, squares, ROWS, col_count, 2, lag_block)
    zero_imag = jnp.where(first, lags[:, :, block_len, :, 0], lags[:, :, 0, :, 1])
    slot_ids = jnp.arange(ROWS, dtype=jnp.int32)[None, None, :, None, None, None]
    part_ids = jnp.arange(2, dtype=jnp.int32)[None, None, None, None, :, None]
    lags = jnp.where(
        (slot_ids == 0) & (part_ids == 1), zero_imag[:, :, None, :, None, :], lags
    )[:, :, :block_len]

    slot_count = (2 * pairs + row_count - 1) // row_count
    owners = jnp.arange(row_count, dtype=jnp.int32)
    owned = band_owner[None, :] == owners[:, None]
    counts = jnp.sum(owned.astype(jnp.int32), axis=1)
    order = jnp.arange(pairs, dtype=jnp.int32)
    starts = jnp.min(jnp.where(owned, order[None, :], pairs - 1), axis=1)
    source = starts[:, None] + jnp.arange(slot_count, dtype=jnp.int32)[None, :]
    source = jnp.minimum(source, pairs - 1).reshape(-1)
    ready = lags.transpose(0, 3, 1, 2, 4, 5).reshape(
        pairs, col_count, squares, block_len * 2 * lag_block
    )
    placed = jnp.take(ready, source, axis=0, mode="clip")
    placed = placed.reshape(row_count, slot_count, col_count, squares, -1)
    placed = placed.transpose(0, 2, 1, 3, 4).reshape(devices, slot_count * squares, -1)
    arrived = lax.all_to_all(placed, ("gy", "gx"), split_axis=0, concat_axis=0, tiled=True)
    arrived = arrived.transpose(1, 0, 2)

    table_span = jnp.asarray(span_table(lag_z, devices, block_len))
    own_count = lax.dynamic_slice_in_dim(counts, row_id, 1)
    return pl.pallas_call(
        functools.partial(spread_kernel, 2 * block_len, norm_scale),
        grid_spec=pltpu.PrefetchScalarGridSpec(
            num_scalar_prefetch=1,
            grid=(slot_count,),
            in_specs=[
                pl.BlockSpec((squares, devices, arrived.shape[2]), lambda s, *_: (s, 0, 0)),
                pl.BlockSpec(table_span.shape, lambda s, *_: (0, 0)),
            ],
            out_specs=pl.BlockSpec((1, squares, lag_block, lag_z), lambda s, *_: (s, 0, 0, 0)),
        ),
        out_shape=jax.ShapeDtypeStruct((slot_count, squares, lag_block, lag_z), jnp.float32),
        compiler_params=pltpu.CompilerParams(vmem_limit_bytes=32 * 2**20),
        name="span_lags",
    )(own_count, arrived, table_span)


def solution(mesh):
    placed = (P(None, "gy", "gx", None), P(), P(), P())
    return jax.shard_map(
        per_device, mesh=mesh, in_specs=placed, out_specs=P("gy", None, "gx", None), check_vma=False
    )
```

time: 2050 us -> 768 us (0.37)
  local copies, waits for them, and re-layouts: 560 us -> 91.3 us
  waiting for transfers between devices: 942 us -> 495 us
  matrix products: 315 us -> 47.4 us
  other arithmetic: 205 us -> 10.6 us
  Pallas kernels: 0 us -> 105 us
    all_to_all x1, waiting for transfers between devices: 707 us -> 182 us  [per_device(): lax.all_to_all(placed, ('gy', 'gx'), split_axis=0, concat_axis=0, tiled=T...]
    dot_general x10 -> x3, matrix products: 315 us -> 47.4 us  [the longest x1 28.7 us: per_device(): lax.dot_general(table_z, velocity.reshape(comps * planes_dev * x_dev, wid...]
    reshape x9 -> x5, local copies, waits for them, and re-layouts: 252 us -> 64.5 us  [the longest x2 24.2 us: per_device(): placed.transpose(0, 2, 1, 3, 4).reshape(devices, slot_count * squares, -1)]
    pallas_call x0 -> x2, Pallas kernels: none -> 105 us  [the longest x1 87 us: per_device(): pl.pallas_call(functools.partial(fold_kernel, comps, planes_dev, block_le...]
    gather x4 -> x1, local copies, waits for them, and re-layouts: 95.2 us -> 12.5 us  [per_device(): placed = jnp.take(ready, source, axis=0, mode='clip')]
    all_to_all x1, waiting for transfers between devices: 235 us -> 313 us  [per_device(): lax.all_to_all(parcels, ('gy', 'gx'), split_axis=0, concat_axis=0, tiled=...]
    dot_general x2 -> x0, other arithmetic: 73.6 us -> none  [the longest x1 37 us: x_transform(): jnp.dot(flat_rows, sin_x, preferred_element_type=jnp.float32)]
    transpose x3 -> x0, local copies, waits for them, and re-layouts: 49.4 us -> none  [the longest x2 43.2 us: spread_right(): return right.transpose(1, 2, 0, 3, 4, 5, 6)[:, :, None]]
  transfers between devices with their start and end apart: 2 -> 2, of which waited for: 2 -> 2; matrix products, arithmetic and copies ran while one was open for 4% -> 0% of each run, Pallas kernels for 0% -> 0%
where the time goes in v1:
time: 768 us; the launch traced here: 760 us
  waiting for transfers between devices  495 us (64%)
  Pallas kernels  105 us (14%)
  local copies, waits for them, and re-layouts  91.3 us (12%)
  matrix products  47.4 us (6%)
  other arithmetic  10.6 us (1%)
  starting transfers between devices  10.1 us (1%)
    all_to_all x1, waiting for transfers between devices, per_device(): lax.all_to_all(parcels, ('gy', 'gx'), split_axis=0, concat_axis=0, tiled=...  313 us
    all_to_all x1, waiting for transfers between devices, per_device(): lax.all_to_all(placed, ('gy', 'gx'), split_axis=0, concat_axis=0, tiled=T...  182 us
    pallas_call x1, Pallas kernels, per_device(): pl.pallas_call(functools.partial(fold_kernel, comps, planes_dev, block_le...  87 us
    dot_general x1, matrix products, per_device(): lax.dot_general(table_z, velocity.reshape(comps * planes_dev * x_dev, wid...  28.7 us
    reshape x2, local copies, waits for them, and re-layouts, per_device(): placed.transpose(0, 2, 1, 3, 4).reshape(devices, slot_count * squares, -1)  24.2 us
    reshape x1, local copies, waits for them, and re-layouts, per_device(): lags.astype(jnp.bfloat16)  21.8 us
    reshape x2, local copies, waits for them, and re-layouts, per_device(): lags.transpose(0, 3, 1, 2, 4, 5)  18.5 us
    pallas_call x1, Pallas kernels, per_device(): pl.pallas_call(functools.partial(spread_kernel, 2 * block_len, norm_scale...  17.8 us
  transfers between devices with their start and end apart: 2, of which 2 were waited for; matrix products, arithmetic and copies ran while one was open for 0% of the time, Pallas kernels for 0%

profile of v1, /device:TPU:17, one launch (start us, length us, event | category | flops | bytes accessed | tf_op | source)
XLA Modules:
  0.0 759.8 jit_solution(2517447862476039324)
XLA Ops:
  0.0 28.7 %convolution_convert_fusion = bf16[1536,4608]{1,0:T(8,128)(2,1)} fusion(bf16[1536,1536]{1,0:T(8,128)(2,1)} %constant.39.clone, bf16[4608,1536]{1,0:T(8,128)(2,1)} %bitcast.31), kind=kOutput, calls=%fused_computation.1 | convolution fusion | flops 21750349824 | bytes 33030144 | tf_op jit(solution)/shard_map/dot_general | solution.py:153
  28.7 6.3 all-to-all-start
  35.0 0.1 select_reduce_fusion
  35.2 0.1 reshape.109
  35.3 0.1 broadcast_and_fusion
  35.4 313.0 %all-to-all-done.got = bf16[32,48,4608]{2,1,0:T(8,128)(2,1)} async-done(((bf16[32,48,4608]{2,1,0:T(8,128)(2,1)}), bf16[32,48,4608]{2,1,0:T(8,128)(2,1)}, u32[]{:S(2)}, u32[]{:S(2)}) %all-to-all-start) | async-done | bytes 14155808 | tf_op jit(solution)/shard_map/all_to_all | solution.py:160
  348.4 0.7 broadcast_in_dim.47.weight_ref
  349.1 87.0 %transform_and_fold.1 = f32[2,48,9,8,384]{4,3,2,1,0:T(8,128)} custom-call(s32[6]{0:T(128)} %refs.1, s32[8]{0:T(128)} %offs.1, bf16[32,48,4608]{2,1,0:T(8,128)(2,1)} %all-to-all-done.got, bf16[1536,1536]{1,0:T(8,128)(2,1)} %constant.40.clone.cos_ref, bf16[1536,1536]{1,0:T(8,128)(2,1)} %constant.41.clone.sin_ref, f32[24,512]{1,0:T(8,128)} %broadcast_in_dim.47.weight_ref), custom_call_target="tpu_custom_call" | custom-call | tf_op jit(solution)/shard_map/transform_and_fold/pallas_call | solution.py:177
  436.1 4.9 fusion.2
  441.0 8.4 %fusion.4 = f32[3456,768]{1,0:T(8,128)S(1)} fusion(f32[3456,384]{1,0:T(8,128)S(1)} %bitcast.28, f32[384,768]{1,0:T(8,128)S(1)} %copy-done.2), kind=kOutput, calls=%fused_computation.19 | convolution fusion | flops 6115295232 | bytes 17104896 | tf_op jit(solution)/shard_map/dot_general | solution.py:211
  449.5 10.3 %add_convert_fusion = bf16[3456,768]{1,0:T(8,128)(2,1)} fusion(f32[3456,768]{1,0:T(8,128)S(1)} %fusion.4, f32[3456,384]{1,0:T(8,128)S(1)} %bitcast.27, f32[384,768]{1,0:T(8,128)S(1)} %copy-done.1), kind=kOutput, calls=%fused_computation.2 | convolution fusion | flops 6120603648 | bytes 22413312 | tf_op jit(solution)/shard_map/dot_general | solution.py:211
  459.7 21.8 %reshape.103 = bf16[48,9,8,4,2,96]{5,4,3,2,1,0:T(2,128)(2,1)} reshape(bf16[3456,768]{1,0:T(8,128)(2,1)} %add_convert_fusion) | data formatting | bytes 10616832 | tf_op jit(solution)/shard_map/reshape | solution.py:214
  481.6 3.0 fusion.3
  484.6 10.3 %fusion = bf16[48,4,9,6,2,96]{5,4,3,0,2,1:T(2,128)(2,1)} fusion(pred[6,2]{1,0:T(8,128)(4,1)S(1)} %bitcast.30, bf16[48,9,8,4,2,96]{5,4,3,2,1,0:T(2,128)(2,1)} %reshape.103, bf16[48,9,1,4,1,96]{5,4,3,2,1,0:T(2,128)(2,1)S(1)} %get-tuple-element.10, bf16[48,9,1,4,1,96]{5,4,3,2,1,0:T(2,128)(2,1)S(1)} %get-tuple-element.9, pred[]{:T(512)S(6)} %eq.37), kind=kLoop, calls=%fused_computation.5 | loop fusion | flops 2156544 | bytes 9953293 | tf_op jit(solution)/shard_map/transpose | solution.py:230
  494.9 12.8 %reshape.104 = bf16[48,4,9,1152]{3,0,2,1:T(8,128)(2,1)} reshape(bf16[48,4,9,6,2,96]{5,4,3,0,2,1:T(2,128)(2,1)} %fusion) | data formatting | bytes 7962624 | tf_op jit(solution)/shard_map/reshape | solution.py:230
  507.8 5.6 copy.43
  513.4 12.5 %gather_fusion = bf16[96,4,9,1152]{3,1,2,0:T(4,128)(2,1)} fusion(bf16[48,4,9,1152]{3,1,2,0:T(4,128)(2,1)} %copy.43, s32[1024]{0:T(1024)S(1)} %pad_clamp_fusion), kind=kCustom, calls=%fused_computation | custom fusion | bytes 15925632 | tf_op jit(solution)/shard_map/jit(_take)/gather | solution.py:233
  525.9 9.8 %copy.47 = bf16[8,4,12,9,1152]{4,3,2,1,0:T(8,128)(2,1)} copy(bf16[8,4,12,9,1152]{4,1,3,2,0:T(4,128)(2,1)} %bitcast.26) | data formatting | bytes 15925248 | tf_op jit(solution)/shard_map/reshape | solution.py:235
  535.7 14.4 %reshape.116 = bf16[32,108,1152]{2,1,0:T(8,128)(2,1)} reshape(bf16[8,4,12,9,1152]{4,3,2,1,0:T(8,128)(2,1)} %copy.47) | data formatting | bytes 15925248 | tf_op jit(solution)/shard_map/reshape | solution.py:235
  550.1 3.8 all-to-all-start.1
  554.0 0.6 dynamic_slice.3.count
  554.6 182.0 %all-to-all-done.1 = bf16[32,108,1152]{2,1,0:T(8,128)(2,1)} async-done(((bf16[32,108,1152]{2,1,0:T(8,128)(2,1)}), bf16[32,108,1152]{2,1,0:T(8,128)(2,1)}, u32[]{:S(2)}, u32[]{:S(2)}) %all-to-all-start.1) | async-done | bytes 7962656 | tf_op jit(solution)/shard_map/all_to_all | solution.py:236
  736.6 5.0 copy.64
  741.5 17.8 %span_lags.1 = f32[12,9,96,384]{3,2,1,0:T(8,128)} custom-call(s32[1]{0:T(128)} %dynamic_slice.3.count, bf16[108,32,1152]{2,1,0:T(8,128)(2,1)S(1)} %bitcast.25, bf16[384,384]{1,0:T(8,128)(2,1)S(1)} %copy-done), custom_call_target="tpu_custom_call" | custom-call | tf_op jit(solution)/shard_map/span_lags/pallas_call | solution.py:241
  (15 shorter events, 0.1 us)
Async XLA Ops:
  28.7 6.3 copy-start.3
  28.7 6.7 copy-start.4
  28.7 319.8 %all-to-all-start = ((bf16[32,48,4608]{2,1,0:T(8,128)(2,1)}), bf16[32,48,4608]{2,1,0:T(8,128)(2,1)}, u32[]{:S(2)}, u32[]{:S(2)}) async-start(bf16[32,48,4608]{2,1,0:T(8,128)(2,1)} %bitcast.29), calls=%async_computation | async-start | bytes 28311552 | tf_op jit(solution)/shard_map/all_to_all | solution.py:160
  436.1 4.9 copy-start.2
  441.0 8.5 %copy-start.1 = (f32[384,768]{1,0:T(8,128)S(1)}, f32[384,768]{1,0:T(8,128)}, u32[]{:S(2)}) copy-start(f32[384,768]{1,0:T(8,128)} %constant.45.clone) | copy-start | bytes 3538948
  550.1 186.5 %all-to-all-start.1 = ((bf16[32,108,1152]{2,1,0:T(8,128)(2,1)}), bf16[32,108,1152]{2,1,0:T(8,128)(2,1)}, u32[]{:S(2)}, u32[]{:S(2)}) async-start(bf16[32,108,1152]{2,1,0:T(8,128)(2,1)} %reshape.116), calls=%async_computation.1 | async-start | bytes 16515072 | tf_op jit(solution)/shard_map/all_to_all | solution.py:236
  554.6 186.9 %copy-start = (bf16[384,384]{1,0:T(8,128)(2,1)S(1)}, bf16[384,384]{1,0:T(8,128)(2,1)}, u32[]{:S(2)}) copy-start(bf16[384,384]{1,0:T(8,128)(2,1)} %constant.46.clone.table) | copy-start | bytes 884740
